TPU v7x, 32 devices: a whole 2x2x4 slice. The times are simulated.
32 devices in a mesh: section: 2 (over core), expert: 16 (over z, y, x).
Axes of the slice: x: 2, y: 2, z: 4, core: 2. Of those that a mesh axis runs over, the one named last changes fastest.
Arguments:
- hidden: bfloat16 [2, 2048, 2048], P('section', 'expert'), may hold values from -6 to 6
- out_grad: bfloat16 [2, 2048, 2048], P('section', 'expert'), may hold values from -6 to 6
- expert_ids: int32 [2, 2048, 8], P('section', 'expert'), may hold values from 0 to 15, all different within a row; in each aligned block of 128 rows (0 to 127, 128 to 255, ..., all dimensions but the last counted through in order) at most 80 rows name the same one
- gate_weight: bfloat16 [2, 2048, 8], P('section', 'expert'), may hold values from 0.029907227 to 0.5
- w_gate: bfloat16 [2, 16, 2048, 768], P('section', 'expert'), may hold values from -0.125 to 0.125
- w_up: bfloat16 [2, 16, 2048, 768], P('section', 'expert'), may hold values from -0.125 to 0.125
- w_down: bfloat16 [2, 16, 768, 2048], P('section', 'expert'), may hold values from -0.21875 to 0.21875
Outputs:
- grad_prev: bfloat16 [2, 2048, 2048], P('section', 'expert')
- grad_gate: bfloat16 [2, 2048, 8], P('section', 'expert')
- grad_w_gate: bfloat16 [2, 16, 2048, 768], P('section', 'expert')
- grad_w_up: bfloat16 [2, 16, 2048, 768], P('section', 'expert')
- grad_w_down: bfloat16 [2, 16, 768, 2048], P('section', 'expert')
Inputs may be any that keep to these rules, and one draw needn't show every extreme that they name: `expert_ids`: each token names 8 different experts. In each layer the 128 tokens of one device (aligned blocks of 128 rows) name one expert at most 80 times, and in every draw some device names some expert exactly 80 times.
All inputs are finite; a program needn't handle non-finite values.
Results may differ from a plain program's by a relative error of at most 0.008.
Values may be sent and summed in bfloat16 or wider, within the bound.
A program may use at most 192 MiB of HBM per device.

v0:
```python
import jax
import jax.numpy as jnp
from jax import lax
from jax.sharding import PartitionSpec as P

ROWBLK = 128


def passed_along(block, axis, distance):
    devices = range(lax.axis_size(axis))
    route = [(i - distance, i) for i in devices if i - distance in devices]
    return lax.ppermute(block, axis, route)


def expert_rows(x_rows, dy_rows, g_rows, w_gate_e, w_up_e, w_down_e):
    pre_gate = jnp.dot(x_rows, w_gate_e, preferred_element_type=jnp.float32)
    pre_up = jnp.dot(x_rows, w_up_e, preferred_element_type=jnp.float32)
    sigma = jax.nn.sigmoid(pre_gate)
    active = pre_gate * sigma
    hidden_rows = (active * pre_up).astype(jnp.bfloat16)
    backward = jnp.dot(dy_rows, w_down_e.T, preferred_element_type=jnp.float32)
    gate_grad = jnp.sum(hidden_rows.astype(jnp.float32) * backward, axis=1).astype(jnp.bfloat16)
    scale = g_rows.astype(jnp.float32)[:, None]
    scaled_dy = (scale * dy_rows.astype(jnp.float32)).astype(jnp.bfloat16)
    grad_hidden = scale * backward
    grad_a = (grad_hidden * pre_up * sigma * (1.0 + pre_gate * (1.0 - sigma))).astype(jnp.bfloat16)
    grad_b = (grad_hidden * active).astype(jnp.bfloat16)
    row_grad = (
        jnp.dot(grad_a, w_gate_e.T, preferred_element_type=jnp.float32)
        + jnp.dot(grad_b, w_up_e.T, preferred_element_type=jnp.float32)
    ).astype(jnp.bfloat16)
    sum_gate = jnp.dot(x_rows.T, grad_a, preferred_element_type=jnp.float32)
    sum_up = jnp.dot(x_rows.T, grad_b, preferred_element_type=jnp.float32)
    sum_down = jnp.dot(hidden_rows.T, scaled_dy, preferred_element_type=jnp.float32)
    return (row_grad, gate_grad, sum_gate, sum_up, sum_down)


def on_device(hidden, out_grad, expert_ids, gate_weight, w_gate, w_up, w_down):
    peers = lax.axis_size("expert")
    x_local = hidden[0]
    dy_local = out_grad[0]
    ids = expert_ids[0]
    gates = gate_weight[0]
    tok_dev, topk = ids.shape
    width = x_local.shape[1]
    slot = min(tok_dev, tok_dev * topk // peers + tok_dev // 8)
    flat = ids.reshape(-1)
    hits = (flat[:, None] == jnp.arange(peers, dtype=jnp.int32)[None, :]).astype(jnp.int32)
    rank = jnp.sum((jnp.cumsum(hits, axis=0) - 1) * hits, axis=1)
    target = flat * slot + rank
    x_routes = jnp.broadcast_to(x_local[:, None, :], (tok_dev, topk, width)).reshape(-1, width)
    dy_routes = jnp.broadcast_to(dy_local[:, None, :], (tok_dev, topk, width)).reshape(-1, width)
    send_x = (
        jnp.zeros((peers * slot, width), jnp.bfloat16)
        .at[target]
        .set(x_routes)
        .reshape(peers, slot, width)
    )
    send_dy = (
        jnp.zeros((peers * slot, width), jnp.bfloat16)
        .at[target]
        .set(dy_routes)
        .reshape(peers, slot, width)
    )
    send_g = (
        jnp.zeros((peers * slot,), jnp.bfloat16)
        .at[target]
        .set(gates.reshape(-1))
        .reshape(peers, slot)
    )
    recv_x, recv_dy, recv_g = (
        lax.all_to_all(send_x, "expert", split_axis=0, concat_axis=0, tiled=True),
        lax.all_to_all(send_dy, "expert", split_axis=0, concat_axis=0, tiled=True),
        lax.all_to_all(send_g, "expert", split_axis=0, concat_axis=0, tiled=True),
    )
    w_gate_e = w_gate[0, 0]
    w_up_e = w_up[0, 0]
    w_down_e = w_down[0, 0]
    units = w_gate_e.shape[1]
    rows = peers * slot
    flat_x = recv_x.reshape(rows, width)
    flat_dy = recv_dy.reshape(rows, width)
    flat_g = recv_g.reshape(rows)
    live = (flat_g > 0).astype(jnp.int32)
    order = jnp.cumsum(live) - 1
    count = jnp.sum(live)
    padded = -(-rows // ROWBLK) * ROWBLK
    place = jnp.where(live > 0, order, padded)
    packed_x = jnp.zeros((padded, width), jnp.bfloat16).at[place].set(flat_x, mode="drop")
    packed_dy = jnp.zeros((padded, width), jnp.bfloat16).at[place].set(flat_dy, mode="drop")
    packed_g = jnp.zeros((padded,), jnp.bfloat16).at[place].set(flat_g, mode="drop")
    blocks = (count + ROWBLK - 1) // ROWBLK

    def block_step(index, carry):
        acc_gate, acc_up, acc_down, out_rows, out_gates = carry
        start = index * ROWBLK
        x_block = lax.dynamic_slice_in_dim(packed_x, start, ROWBLK, 0)
        dy_block = lax.dynamic_slice_in_dim(packed_dy, start, ROWBLK, 0)
        g_block = lax.dynamic_slice_in_dim(packed_g, start, ROWBLK, 0)
        row_grad, gate_grad, sum_gate, sum_up, sum_down = expert_rows(
            x_block, dy_block, g_block, w_gate_e, w_up_e, w_down_e
        )
        out_rows = lax.dynamic_update_slice_in_dim(out_rows, row_grad, start, 0)
        out_gates = lax.dynamic_update_slice_in_dim(out_gates, gate_grad, start, 0)
        return (acc_gate + sum_gate, acc_up + sum_up, acc_down + sum_down, out_rows, out_gates)

    start_carry = (
        jnp.zeros((width, units), jnp.float32),
        jnp.zeros((width, units), jnp.float32),
        jnp.zeros((units, width), jnp.float32),
        jnp.zeros((padded, width), jnp.bfloat16),
        jnp.zeros((padded,), jnp.bfloat16),
    )
    acc_gate, acc_up, acc_down, out_rows, out_gates = lax.fori_loop(
        0, blocks, block_step, start_carry
    )
    back_rows = jnp.take(out_rows, place, axis=0, mode="fill", fill_value=0).reshape(
        peers, slot, width
    )
    back_gates = jnp.take(out_gates, place, axis=0, mode="fill", fill_value=0).reshape(peers, slot)
    ret_rows, ret_gates = (
        lax.all_to_all(back_rows, "expert", split_axis=0, concat_axis=0, tiled=True),
        lax.all_to_all(back_gates, "expert", split_axis=0, concat_axis=0, tiled=True),
    )
    token_rows = ret_rows.reshape(rows, width)[target].reshape(tok_dev, topk, width)
    grad_in = jnp.sum(token_rows.astype(jnp.float32), axis=1).astype(jnp.bfloat16)
    grad_gate = ret_gates.reshape(rows)[target].reshape(tok_dev, topk)
    grad_prev = passed_along(grad_in, "section", -1)
    return (
        grad_prev[None],
        grad_gate[None],
        acc_gate.astype(jnp.bfloat16)[None, None],
        acc_up.astype(jnp.bfloat16)[None, None],
        acc_down.astype(jnp.bfloat16)[None, None],
    )


def solution(mesh):
    return jax.shard_map(
        on_device,
        mesh=mesh,
        in_specs=(
            P("section", "expert", None),
            P("section", "expert", None),
            P("section", "expert", None),
            P("section", "expert", None),
            P("section", "expert", None, None),
            P("section", "expert", None, None),
            P("section", "expert", None, None),
        ),
        out_specs=(
            P("section", "expert", None),
            P("section", "expert", None),
            P("section", "expert", None, None),
            P("section", "expert", None, None),
            P("section", "expert", None, None),
        ),
        check_vma=False,
    )
```

profile of v0, /device:TPU:1, one launch (start us, length us, event | category | flops | bytes accessed | tf_op | source)
XLA Modules:
  0.0 744.1 jit_solution(11324530929247251300)
XLA Ops:
  3.5 4.5 reduce-window.15
  8.5 7.6 %scatter_custom_fusion = bf16[1280]{0:T(1024)(128)(2,1)S(1)} fusion(s32[1024]{0:T(1024)S(1)} %bitcast.111, bf16[1024]{0:T(1024)(128)(2,1)S(1)} %reshape.278, bf16[]{:T(256)} %constant.52.clone.1), kind=kCustom, calls=%fused_computation.81 | custom fusion | bytes 2562 | tf_op jit(solution)/shard_map/scatter | solution.py:68
  16.8 7.4 all-to-all-start
  24.2 9.6 %scatter_custom_fusion.4 = bf16[1280,2048]{1,0:T(8,128)(2,1)} fusion(s32[1024]{0:T(1024)S(1)} %bitcast.112, bf16[]{:T(256)} %constant.52.clone.1, bf16[128,2048]{1,0:T(8,128)(2,1)S(1)} %bitcast.94), kind=kCustom, calls=%fused_computation.42 | custom fusion | bytes 5767170 | tf_op jit(solution)/shard_map/scatter | solution.py:62
  33.8 7.0 all-to-all-start.2
  40.8 9.7 %scatter_custom_fusion.1 = bf16[1280,2048]{1,0:T(8,128)(2,1)} fusion(s32[1024]{0:T(1024)S(1)} %bitcast.113, bf16[]{:T(256)} %constant.52.clone.1, bf16[128,2048]{1,0:T(8,128)(2,1)S(1)} %bitcast.106), kind=kCustom, calls=%fused_computation.44 | custom fusion | bytes 5767170 | tf_op jit(solution)/shard_map/scatter | solution.py:56
  50.5 87.0 %all-to-all-done.2 = bf16[16,80,2048]{2,1,0:T(8,128)(2,1)} async-done(((bf16[16,80,2048]{2,1,0:T(8,128)(2,1)}), bf16[16,80,2048]{2,1,0:T(8,128)(2,1)}, u32[]{:S(2)}, u32[]{:S(2)}) %all-to-all-start.2) | async-done | bytes 5242912 | tf_op jit(solution)/shard_map/all_to_all | solution.py:73
  137.5 24.8 %all-to-all-start.1 = ((bf16[16,80,2048]{2,1,0:T(8,128)(2,1)}), bf16[16,80,2048]{2,1,0:T(8,128)(2,1)}, u32[]{:S(2)}, u32[]{:S(2)}) async-start(bf16[16,80,2048]{2,1,0:T(8,128)(2,1)} %bitcast.103), calls=%async_computation.1 | async-start | bytes 10485760 | tf_op jit(solution)/shard_map/all_to_all | solution.py:72
  164.7 12.8 %scatter_custom_fusion.3 = bf16[1280]{0:T(1024)(128)(2,1)S(1)} fusion(s32[1280]{0:T(1024)S(1)} %fusion.34, bf16[1280]{0:T(1024)(128)(2,1)S(1)} %reshape.302, bf16[]{:T(256)} %constant.52.clone.1), kind=kCustom, calls=%fused_computation.79 | custom fusion | bytes 2562 | tf_op jit(solution)/shard_map/scatter | solution.py:91
  177.6 14.0 %scatter_custom_fusion.5 = bf16[1280,2048]{1,0:T(8,128)(2,1)} fusion(s32[1280]{0:T(1024)S(1)} %fusion.34, bf16[1280,2048]{1,0:T(8,128)(2,1)} %bitcast.12, bf16[]{:T(256)} %constant.52.clone.1), kind=kCustom, calls=%fused_computation.49 | custom fusion | bytes 5243392 | tf_op jit(solution)/shard_map/scatter | solution.py:90
  191.6 67.0 %all-to-all-done.1 = bf16[16,80,2048]{2,1,0:T(8,128)(2,1)} async-done(((bf16[16,80,2048]{2,1,0:T(8,128)(2,1)}), bf16[16,80,2048]{2,1,0:T(8,128)(2,1)}, u32[]{:S(2)}, u32[]{:S(2)}) %all-to-all-start.1) | async-done | bytes 5242912 | tf_op jit(solution)/shard_map/all_to_all | solution.py:72
  258.6 14.2 %scatter_custom_fusion.2 = bf16[1280,2048]{1,0:T(8,128)(2,1)} fusion(s32[1280]{0:T(1024)S(1)} %fusion.34, bf16[1280,2048]{1,0:T(8,128)(2,1)} %bitcast.8, bf16[]{:T(256)} %constant.52.clone.1), kind=kCustom, calls=%fused_computation.52 | custom fusion | bytes 5243392 | tf_op jit(solution)/shard_map/scatter | solution.py:89
  285.2 261.8 %while.18 = (s32[]{:T(128)}, f32[2048,768]{1,0:T(8,128)}, f32[2048,768]{1,0:T(8,128)}, f32[768,2048]{1,0:T(8,128)}, bf16[1280,2048]{1,0:T(8,128)(2,1)}, /*index=...) while((s32[]{:T(128)}, f32[2048,768]{1,0:T(8,128)}, ...), condition=%wide.region_14.15_spmd, body=%wide.region_12.14_spmd.sunk | while | flops 3229122560 | bytes 207096816 | solution.py:114
  547.0 14.0 %gather_fusion = bf16[1280,2048]{1,0:T(8,128)(2,1)} fusion(bf16[1280,2048]{1,0:T(8,128)(2,1)} %get-tuple-element.77, s32[2048]{0:T(1024)S(1)} %pad_clamp_fusion), kind=kCustom, calls=%fused_computation | custom fusion | bytes 10490880 | tf_op jit(solution)/shard_map/jit(_take)/gather | solution.py:117
  561.0 5.2 broadcast_select_fusion
  566.2 23.3 %all-to-all-start.3 = ((bf16[16,80,2048]{2,1,0:T(8,128)(2,1)}), bf16[16,80,2048]{2,1,0:T(8,128)(2,1)}, u32[]{:S(2)}, u32[]{:S(2)}) async-start(bf16[16,80,2048]{2,1,0:T(8,128)(2,1)} %broadcast_select_fusion), calls=%async_computation.3 | async-start | bytes 10485760 | tf_op jit(solution)/shard_map/all_to_all | solution.py:122
  589.7 8.0 %gather_fusion.2 = bf16[1280]{0:T(1024)(128)(2,1)S(1)} fusion(bf16[1280]{0:T(1024)(128)(2,1)S(1)} %get-tuple-element.78, s32[2048]{0:T(1024)S(1)} %pad_clamp_fusion), kind=kCustom, calls=%fused_computation.2 | custom fusion | bytes 10240 | tf_op jit(solution)/shard_map/jit(_take)/gather | solution.py:120
  598.4 7.9 %convert_bitcast_fusion.1 = (bf16[1,1,2048,768]{3,2,1,0:T(8,128)(2,1)}, bf16[1,1,2048,768]{3,2,1,0:T(8,128)(2,1)}) fusion(f32[2048,768]{1,0:T(8,128)} %get-tuple-element.80, f32[2048,768]{1,0:T(8,128)} %get-tuple-element.79), kind=kLoop, calls=%fused_computation.47 | loop fusion | flops 3145728 | bytes 18874368 | tf_op jit(solution)/shard_map/broadcast_in_dim | solution.py:133
  606.3 79.7 %all-to-all-done.3 = bf16[16,80,2048]{2,1,0:T(8,128)(2,1)} async-done(((bf16[16,80,2048]{2,1,0:T(8,128)(2,1)}), bf16[16,80,2048]{2,1,0:T(8,128)(2,1)}, u32[]{:S(2)}, u32[]{:S(2)}) %all-to-all-start.3) | async-done | bytes 5242912 | tf_op jit(solution)/shard_map/all_to_all | solution.py:122
  686.0 23.4 %all-to-all-start.4 = ((bf16[16,1,80]{2,1,0:T(2,128)(2,1)}), bf16[16,1,80]{2,1,0:T(2,128)(2,1)S(1)}, u32[]{:S(2)}, u32[]{:S(2)}) async-start(bf16[16,1,80]{2,1,0:T(2,128)(2,1)} %copy.37), calls=%async_computation.4 | async-start | bytes 16384 | tf_op jit(solution)/shard_map/all_to_all | solution.py:123
  709.4 12.0 %gather_fusion.1 = bf16[1024,2048]{1,0:T(8,128)(2,1)} fusion(bf16[1280,2048]{1,0:T(8,128)(2,1)} %bitcast.17, s32[1024]{0:T(1024)S(1)} %broadcast_clamp_fusion), kind=kCustom, calls=%fused_computation.1 | custom fusion | bytes 8392704 | tf_op jit(solution)/shard_map/gather | solution.py:125
  721.4 5.1 bitcast_reduce_fusion
  730.2 5.0 convert_bitcast_fusion
  735.3 6.8 gather_fusion.3
  (389 shorter events, 284.2 us)
Async XLA Ops:
  0.6 23.6 %copy-start = (bf16[1,128,2048]{2,1,0:T(8,128)(2,1)S(1)}, bf16[1,128,2048]{2,1,0:T(8,128)(2,1)}, u32[]{:S(2)}) copy-start(bf16[1,128,2048]{2,1,0:T(8,128)(2,1)} %param.10) | copy-start | bytes 1572868
  16.8 17.1 %all-to-all-start = ((bf16[16,1,80]{2,1,0:T(2,128)(2,1)}), bf16[16,1,80]{2,1,0:T(2,128)(2,1)S(1)}, u32[]{:S(2)}, u32[]{:S(2)}) async-start(bf16[16,1,80]{2,1,0:T(2,128)(2,1)} %all_to_all.25), calls=%async_computation | async-start | bytes 16384 | tf_op jit(solution)/shard_map/all_to_all | solution.py:74
  33.8 103.7 %all-to-all-start.2 = ((bf16[16,80,2048]{2,1,0:T(8,128)(2,1)}), bf16[16,80,2048]{2,1,0:T(8,128)(2,1)}, u32[]{:S(2)}, u32[]{:S(2)}) async-start(bf16[16,80,2048]{2,1,0:T(8,128)(2,1)} %bitcast.104), calls=%async_computation.2 | async-start | bytes 10485760 | tf_op jit(solution)/shard_map/all_to_all | solution.py:73
  137.5 121.1 %all-to-all-start.1 = ((bf16[16,80,2048]{2,1,0:T(8,128)(2,1)}), bf16[16,80,2048]{2,1,0:T(8,128)(2,1)}, u32[]{:S(2)}, u32[]{:S(2)}) async-start(bf16[16,80,2048]{2,1,0:T(8,128)(2,1)} %bitcast.103), calls=%async_computation.1 | async-start | bytes 10485760 | tf_op jit(solution)/shard_map/all_to_all | solution.py:72
  290.8 10.0 %slice-start.4 = ((s8[6291456]{0:T(1024)(128)(4,1)}), s8[2097152]{0:T(1024)(128)(4,1)S(1)}, s32[]{:S(2)}) async-start(s8[6291456]{0:T(1024)(128)(4,1)} %bitcast.101), calls=%async_computation.9 | async-start | bytes 4194304 | tf_op jit(solution)/shard_map/while
  296.8 9.2 %slice-start.2 = ((s8[6291456]{0:T(1024)(128)(4,1)}), s8[4194304]{0:T(1024)(128)(4,1)S(1)}, s32[]{:S(2)}) async-start(s8[6291456]{0:T(1024)(128)(4,1)} %bitcast.99), calls=%async_computation.7 | async-start | bytes 8388608 | tf_op jit(solution)/shard_map/while
  317.0 10.1 %slice-start.4 = ((s8[6291456]{0:T(1024)(128)(4,1)}), s8[2097152]{0:T(1024)(128)(4,1)S(1)}, s32[]{:S(2)}) async-start(s8[6291456]{0:T(1024)(128)(4,1)} %bitcast.101), calls=%async_computation.9 | async-start | bytes 4194304 | tf_op jit(solution)/shard_map/while
  323.0 9.2 %slice-start.2 = ((s8[6291456]{0:T(1024)(128)(4,1)}), s8[4194304]{0:T(1024)(128)(4,1)S(1)}, s32[]{:S(2)}) async-start(s8[6291456]{0:T(1024)(128)(4,1)} %bitcast.99), calls=%async_computation.7 | async-start | bytes 8388608 | tf_op jit(solution)/shard_map/while
  343.2 10.0 %slice-start.4 = ((s8[6291456]{0:T(1024)(128)(4,1)}), s8[2097152]{0:T(1024)(128)(4,1)S(1)}, s32[]{:S(2)}) async-start(s8[6291456]{0:T(1024)(128)(4,1)} %bitcast.101), calls=%async_computation.9 | async-start | bytes 4194304 | tf_op jit(solution)/shard_map/while
  369.3 10.0 %slice-start.4 = ((s8[6291456]{0:T(1024)(128)(4,1)}), s8[2097152]{0:T(1024)(128)(4,1)S(1)}, s32[]{:S(2)}) async-start(s8[6291456]{0:T(1024)(128)(4,1)} %bitcast.101), calls=%async_computation.9 | async-start | bytes 4194304 | tf_op jit(solution)/shard_map/while
  375.3 9.2 %slice-start.2 = ((s8[6291456]{0:T(1024)(128)(4,1)}), s8[4194304]{0:T(1024)(128)(4,1)S(1)}, s32[]{:S(2)}) async-start(s8[6291456]{0:T(1024)(128)(4,1)} %bitcast.99), calls=%async_computation.7 | async-start | bytes 8388608 | tf_op jit(solution)/shard_map/while
  395.5 10.0 %slice-start.4 = ((s8[6291456]{0:T(1024)(128)(4,1)}), s8[2097152]{0:T(1024)(128)(4,1)S(1)}, s32[]{:S(2)}) async-start(s8[6291456]{0:T(1024)(128)(4,1)} %bitcast.101), calls=%async_computation.9 | async-start | bytes 4194304 | tf_op jit(solution)/shard_map/while
  401.5 9.2 %slice-start.2 = ((s8[6291456]{0:T(1024)(128)(4,1)}), s8[4194304]{0:T(1024)(128)(4,1)S(1)}, s32[]{:S(2)}) async-start(s8[6291456]{0:T(1024)(128)(4,1)} %bitcast.99), calls=%async_computation.7 | async-start | bytes 8388608 | tf_op jit(solution)/shard_map/while
  421.7 10.0 %slice-start.4 = ((s8[6291456]{0:T(1024)(128)(4,1)}), s8[2097152]{0:T(1024)(128)(4,1)S(1)}, s32[]{:S(2)}) async-start(s8[6291456]{0:T(1024)(128)(4,1)} %bitcast.101), calls=%async_computation.9 | async-start | bytes 4194304 | tf_op jit(solution)/shard_map/while
  427.7 9.2 %slice-start.2 = ((s8[6291456]{0:T(1024)(128)(4,1)}), s8[4194304]{0:T(1024)(128)(4,1)S(1)}, s32[]{:S(2)}) async-start(s8[6291456]{0:T(1024)(128)(4,1)} %bitcast.99), calls=%async_computation.7 | async-start | bytes 8388608 | tf_op jit(solution)/shard_map/while
  447.9 10.0 %slice-start.4 = ((s8[6291456]{0:T(1024)(128)(4,1)}), s8[2097152]{0:T(1024)(128)(4,1)S(1)}, s32[]{:S(2)}) async-start(s8[6291456]{0:T(1024)(128)(4,1)} %bitcast.101), calls=%async_computation.9 | async-start | bytes 4194304 | tf_op jit(solution)/shard_map/while
  474.0 10.0 %slice-start.4 = ((s8[6291456]{0:T(1024)(128)(4,1)}), s8[2097152]{0:T(1024)(128)(4,1)S(1)}, s32[]{:S(2)}) async-start(s8[6291456]{0:T(1024)(128)(4,1)} %bitcast.101), calls=%async_computation.9 | async-start | bytes 4194304 | tf_op jit(solution)/shard_map/while
  500.2 10.0 %slice-start.4 = ((s8[6291456]{0:T(1024)(128)(4,1)}), s8[2097152]{0:T(1024)(128)(4,1)S(1)}, s32[]{:S(2)}) async-start(s8[6291456]{0:T(1024)(128)(4,1)} %bitcast.101), calls=%async_computation.9 | async-start | bytes 4194304 | tf_op jit(solution)/shard_map/while
  506.2 9.2 %slice-start.2 = ((s8[6291456]{0:T(1024)(128)(4,1)}), s8[4194304]{0:T(1024)(128)(4,1)S(1)}, s32[]{:S(2)}) async-start(s8[6291456]{0:T(1024)(128)(4,1)} %bitcast.99), calls=%async_computation.7 | async-start | bytes 8388608 | tf_op jit(solution)/shard_map/while
  526.4 10.0 %slice-start.4 = ((s8[6291456]{0:T(1024)(128)(4,1)}), s8[2097152]{0:T(1024)(128)(4,1)S(1)}, s32[]{:S(2)}) async-start(s8[6291456]{0:T(1024)(128)(4,1)} %bitcast.101), calls=%async_computation.9 | async-start | bytes 4194304 | tf_op jit(solution)/shard_map/while
  566.2 119.7 %all-to-all-start.3 = ((bf16[16,80,2048]{2,1,0:T(8,128)(2,1)}), bf16[16,80,2048]{2,1,0:T(8,128)(2,1)}, u32[]{:S(2)}, u32[]{:S(2)}) async-start(bf16[16,80,2048]{2,1,0:T(8,128)(2,1)} %broadcast_select_fusion), calls=%async_computation.3 | async-start | bytes 10485760 | tf_op jit(solution)/shard_map/all_to_all | solution.py:122
  686.0 49.2 %all-to-all-start.4 = ((bf16[16,1,80]{2,1,0:T(2,128)(2,1)}), bf16[16,1,80]{2,1,0:T(2,128)(2,1)S(1)}, u32[]{:S(2)}, u32[]{:S(2)}) async-start(bf16[16,1,80]{2,1,0:T(2,128)(2,1)} %copy.37), calls=%async_computation.4 | async-start | bytes 16384 | tf_op jit(solution)/shard_map/all_to_all | solution.py:123
  726.5 16.4 %collective-permute-start = (bf16[128,2048]{1,0:T(8,128)(2,1)S(1)}, bf16[128,2048]{1,0:T(8,128)(2,1)S(1)}, u32[]{:S(2)}, u32[]{:S(2)}) collective-permute-start(bf16[128,2048]{1,0:T(8,128)(2,1)S(1)} %bitcast_reduce_fusion), channel_id=1, source_target_pairs={{16,0},{17,1},{18,2},{19,3},{20,4},{21,5},{22,6},{23,7},{24,8},{25... | collective-permute-start | bytes 1572872 | tf_op jit(solution)/shard_map/ppermute | solution.py:12
  730.2 13.5 %copy-start.1 = (bf16[1,128,2048]{2,1,0:T(8,128)(2,1)S(1)}, bf16[1,128,2048]{2,1,0:T(8,128)(2,1)}, u32[]{:S(2)}) copy-start(bf16[1,128,2048]{2,1,0:T(8,128)(2,1)} %param.10) | copy-start | bytes 1572868
  (85 other events, 392.9 us)
where the time goes:
time: 754 us; the launch traced here: 744 us
  waiting for transfers between devices  234 us (31%)
  matrix products  230 us (31%)
  local copies, waits for them, and re-layouts  157 us (21%)
  starting transfers between devices  89.7 us (12%)
  other arithmetic  30.6 us (4%)
    all_to_all x1, waiting for transfers between devices, on_device(): lax.all_to_all(send_dy, 'expert', split_axis=0, concat_axis=0, tiled=True)  87 us
    all_to_all x1, waiting for transfers between devices, on_device(): lax.all_to_all(back_rows, 'expert', split_axis=0, concat_axis=0, tiled=True)  79.7 us
    all_to_all x1, waiting for transfers between devices, on_device(): lax.all_to_all(send_x, 'expert', split_axis=0, concat_axis=0, tiled=True)  67 us
    dot_general x10, matrix products, expert_rows(): jnp.dot(grad_b, w_up_e.T, preferred_element_type=jnp.float32)  40 us
    dot_general x10, matrix products, expert_rows(): jnp.dot(grad_a, w_gate_e.T, preferred_element_type=jnp.float32)  31.8 us
    dot_general x10, matrix products, expert_rows(): pre_gate = jnp.dot(x_rows, w_gate_e, preferred_element_type=jnp.float32)  27.7 us
    dot_general x10, matrix products, expert_rows(): sum_gate = jnp.dot(x_rows.T, grad_a, preferred_element_type=jnp.float32)  27.3 us
    dot_general x10, matrix products, expert_rows(): sum_up = jnp.dot(x_rows.T, grad_b, preferred_element_type=jnp.float32)  27.3 us
  transfers between devices with their start and end apart: 6, of which 3 were waited for; matrix products, arithmetic and copies ran while one was open for 13% of the time, Pallas kernels for 0%

commit v1 on v0

v1 whole, which is shorter than its diff:
```python
import functools

import jax
import jax.numpy as jnp
from jax import lax
from jax.experimental import pallas as pl
from jax.experimental.pallas import tpu as pltpu
from jax.sharding import PartitionSpec as P

MESH = pl.DeviceIdType.MESH
SLOT = 80
BF = jnp.bfloat16
F32 = jnp.float32
NT = (((1,), (1,)), ((), ()))
TN = (((0,), (0,)), ((), ()))


def plane_at(k, z):
    half = z // 2
    zz = z + half * (3 - 2 * z)
    hk = k // 2
    p0 = (1 - hk) * ((k + zz) % 2) + hk * k
    return p0 + half * (3 - 2 * p0)


def kernel(
    x_in, dy_in, ids_t, g_t, wg_in, wu_in, wd_in,
    gin_out, gg_out, dwg_out, dwu_out, dwd_out,
    G, META, Xc, Yc, Dx, Hc, Ac, Bc, wg, wu, wd, GG, RF, RD, RZ, RFg, RDg, RZg, SG, SU, SD,
    load_sem, in_sem, out_sem, in_meta, out_meta,
    rs_in, rs_out, rz_in, rz_out, st_sem,
):
    tok, width = x_in.shape
    units = wg.shape[1]
    sec = lax.axis_index("section")
    me = lax.axis_index("expert")
    z, y, x = me // 4, (me // 2) % 2, me % 2
    cx = y * 2 + (1 - x)
    cy = (1 - y) * 2 + x
    cd = (1 - y) * 2 + (1 - x)
    co = y * 2 + x
    to_x = (sec, z * 4 + cx)
    to_y = (sec, z * 4 + cy)
    to_up = (sec, me + 4)
    to_dn = (sec, me - 4)
    has_up = z < 3
    has_dn = z > 0

    loads = []
    for n, (src, dst) in enumerate(
        ((x_in, G.at[0, me]), (dy_in, G.at[1, me]), (wg_in, wg), (wu_in, wu), (wd_in, wd))
    ):
        c = pltpu.make_async_copy(src, dst, load_sem.at[n])
        c.start()
        loads.append(c)

    experts = lax.broadcasted_iota(jnp.int32, (16, tok), 0)
    hit = jnp.zeros((16, tok), F32)
    gsum = jnp.zeros((16, tok), F32)
    for k in range(ids_t.shape[0]):
        same = (ids_t[k : k + 1, :] == experts).astype(F32)
        hit = hit + same
        gsum = gsum + same * g_t[k : k + 1, :]
    before = (
        lax.broadcasted_iota(jnp.int32, (tok, tok), 0) < lax.broadcasted_iota(jnp.int32, (tok, tok), 1)
    ).astype(BF)
    rank = jnp.dot(hit.astype(BF), before, preferred_element_type=F32)
    rank = jnp.where(hit > 0, rank, -1.0)
    META[me, 0:16, :] = rank.astype(BF)
    META[me, 16:32, :] = gsum.astype(BF)

    barrier = pltpu.get_barrier_semaphore()
    pl.semaphore_signal(barrier, inc=1, device_id=to_x, device_id_type=MESH)
    pl.semaphore_signal(barrier, inc=1, device_id=to_y, device_id_type=MESH)

    @pl.when(has_up)
    def _():
        pl.semaphore_signal(barrier, inc=1, device_id=to_up, device_id_type=MESH)

    @pl.when(has_dn)
    def _():
        pl.semaphore_signal(barrier, inc=1, device_id=to_dn, device_id_type=MESH)

    pl.semaphore_wait(barrier, 2 + (5 - z) // 3 + (z + 2) // 3)

    def block_copy(arr, blk, way, to):
        if arr == 2:
            return pltpu.make_async_remote_copy(
                META.at[blk], META.at[blk], out_meta.at[blk, way], in_meta.at[blk],
                device_id=to, device_id_type=MESH)
        return pltpu.make_async_remote_copy(
            G.at[arr, blk], G.at[arr, blk], out_sem.at[arr, blk, way], in_sem.at[arr, blk],
            device_id=to, device_id_type=MESH)

    def arrive(arr, blk):
        block_copy(arr, blk, 0, to_x).wait_recv()

    loads[0].wait()
    loads[1].wait()

    for arr in (2, 0, 1):
        @pl.when(has_up)
        def _(arr=arr):
            block_copy(arr, me, 2, to_up).start()

        @pl.when(has_dn)
        def _(arr=arr):
            block_copy(arr, me, 3, to_dn).start()

        block_copy(arr, me, 0, to_x).start()
        block_copy(arr, me, 1, to_y).start()
    for c in loads[2:]:
        c.wait()

    def own_step(k):
        p = plane_at(k, z)
        blk = p * 4 + co
        for arr in (2, 0, 1):
            arrive(arr, blk)

            @pl.when((p > z) & has_dn)
            def _(arr=arr):
                block_copy(arr, blk, 3, to_dn).start()

            @pl.when((p < z) & has_up)
            def _(arr=arr):
                block_copy(arr, blk, 2, to_up).start()

            block_copy(arr, blk, 0, to_x).start()
            block_copy(arr, blk, 1, to_y).start()

    def side_step(k):
        p = plane_at(k, z)
        for arr in (2, 0, 1):
            arrive(arr, p * 4 + cx)
            if arr != 1:
                block_copy(arr, p * 4 + cx, 1, to_y).start()
            arrive(arr, p * 4 + cy)
            if arr == 1:
                block_copy(arr, p * 4 + cy, 0, to_x).start()

    expert_row = lax.broadcasted_iota(jnp.int32, (16, tok), 0) == me

    def onehot(blk):
        r = jnp.sum(jnp.where(expert_row, META[blk, 0:16, :].astype(F32), 0.0), axis=0, keepdims=True)
        slots = lax.broadcasted_iota(jnp.int32, (SLOT, tok), 0).astype(F32)
        return (slots == r).astype(F32)

    def group(k):
        p = plane_at(k, z)
        for arr in (2, 0, 1):
            arrive(arr, p * 4 + cd)
        base = k * (4 * SLOT)
        rows = pl.ds(pl.multiple_of(base, 4 * SLOT), 4 * SLOT)
        scales, picks = [], []
        for i, c in enumerate((co, cx, cy, cd)):
            blk = p * 4 + c
            pick = onehot(blk)
            gs = jnp.sum(jnp.where(expert_row, META[blk, 16:32, :].astype(F32), 0.0), axis=0, keepdims=True)
            scales.append(jnp.sum(pick * gs, axis=1, keepdims=True))
            picks.append(pick)
            part = pl.ds(pl.multiple_of(base + i * SLOT, SLOT), SLOT)
            pb = pick.astype(BF)

            def gather(j, _, pb=pb, blk=blk, part=part):
                cols = pl.ds(pl.multiple_of(j * 512, 512), 512)
                Xc[part, cols] = jnp.dot(pb, G[0, blk, :, cols], preferred_element_type=F32).astype(BF)
                Yc[part, cols] = jnp.dot(pb, G[1, blk, :, cols], preferred_element_type=F32).astype(BF)
                return 0

            lax.fori_loop(0, width // 512, gather, 0)
        scale = jnp.concatenate(scales, axis=0)

        def hidden_chunk(j, total):
            cols = pl.ds(pl.multiple_of(j * 256, 256), 256)
            a = jnp.dot(Xc[rows, :], wg[:, cols], preferred_element_type=F32)
            b = jnp.dot(Xc[rows, :], wu[:, cols], preferred_element_type=F32)
            back = lax.dot_general(Yc[rows, :], wd[cols, :], NT, preferred_element_type=F32)
            s = jax.nn.sigmoid(a)
            active = a * s
            h = (active * b).astype(BF)
            Hc[rows, cols] = h
            dh = scale * back
            Ac[rows, cols] = (dh * b * s * (1.0 + a * (1.0 - s))).astype(BF)
            Bc[rows, cols] = (dh * active).astype(BF)
            return total + jnp.sum(h.astype(F32) * back, axis=1, keepdims=True)

        total = lax.fori_loop(0, units // 256, hidden_chunk, jnp.zeros((4 * SLOT, 1), F32))
        for i, c in enumerate((co, cx, cy, cd)):
            row = jnp.sum(picks[i] * total[i * SLOT : (i + 1) * SLOT], axis=0, keepdims=True)
            GG[p * 4 + c] = jnp.where(expert_row, row, 0.0).astype(BF)

        def input_chunk(j, _):
            cols = pl.ds(pl.multiple_of(j * 256, 256), 256)
            Yc[rows, cols] = (scale * Yc[rows, cols].astype(F32)).astype(BF)
            d = lax.dot_general(Ac[rows, :], wg[cols, :], NT, preferred_element_type=F32)
            d = d + lax.dot_general(Bc[rows, :], wu[cols, :], NT, preferred_element_type=F32)
            Dx[rows, cols] = d.astype(BF)
            return 0

        lax.fori_loop(0, width // 256, input_chunk, 0)

    def ag_step(k, _):
        @pl.when(k < 3)
        def _():
            own_step(k + 1)

        @pl.when(k < 4)
        def _():
            side_step(k)

        @pl.when(k > 0)
        def _():
            group(k - 1)

        return 0

    lax.fori_loop(0, 5, ag_step, 0)

    def drain(k, _):
        p = plane_at(k, z)
        blk = p * 4 + co
        for arr in (0, 1, 2):
            block_copy(arr, blk, 0, to_x).wait_send()
            block_copy(arr, blk, 1, to_y).wait_send()

            @pl.when(has_up & (p <= z))
            def _(arr=arr):
                block_copy(arr, blk, 2, to_up).wait_send()

            @pl.when(has_dn & (p >= z))
            def _(arr=arr):
                block_copy(arr, blk, 3, to_dn).wait_send()

            if arr != 1:
                block_copy(arr, p * 4 + cx, 1, to_y).wait_send()
            else:
                block_copy(arr, p * 4 + cy, 0, to_x).wait_send()
        return 0

    lax.fori_loop(0, 4, drain, 0)

    halves = tok // 2
    TOP, LOW = pl.ds(0, halves), pl.ds(halves, halves)

    def back_copy(n, k):
        p = plane_at(k, z)
        src, dst, to = (
            (G.at[0, p * 4 + cd, TOP, :], RD.at[0, k], to_x),
            (G.at[0, p * 4 + cd, LOW, :], RD.at[1, k], to_y),
            (GG.at[p * 4 + cd], RDg.at[k], to_x),
            (G.at[0, p * 4 + cx], RF.at[0, k], to_x),
            (G.at[0, p * 4 + cy], RF.at[1, k], to_y),
            (GG.at[p * 4 + cx], RFg.at[0, k], to_x),
            (GG.at[p * 4 + cy], RFg.at[1, k], to_y),
        )[n]
        return pltpu.make_async_remote_copy(
            src, dst, rs_out.at[n, k], rs_in.at[n, k], device_id=to, device_id_type=MESH)

    def line_copy(n, t, down):
        blk = t * 4 + co
        d = 1 if down else 0
        src, dst = ((G.at[0, blk], RZ.at[d, t]), (GG.at[blk], RZg.at[d, t]))[n]
        return pltpu.make_async_remote_copy(
            src, dst, rz_out.at[n, t], rz_in.at[n, d, t],
            device_id=to_dn if down else to_up, device_id_type=MESH)

    def spread(i, _):
        k = 3 - i
        p = plane_at(k, z)
        for n, c in ((3, cd), (1, cx), (2, cy), (0, co)):
            blk = p * 4 + c
            pb = onehot(blk).astype(BF)
            part = pl.ds(pl.multiple_of(k * (4 * SLOT) + n * SLOT, SLOT), SLOT)

            def put(j, _, pb=pb, blk=blk, part=part):
                cols = pl.ds(pl.multiple_of(j * 512, 512), 512)
                G[0, blk, :, cols] = lax.dot_general(
                    pb, Dx[part, cols], TN, preferred_element_type=F32).astype(BF)
                return 0

            lax.fori_loop(0, width // 512, put, 0)
            if n == 3:
                for m in (0, 1, 2):
                    back_copy(m, k).start()
        return 0

    lax.fori_loop(0, 4, spread, 0)

    def second(k):
        p = plane_at(k, z)
        for n in (0, 1, 2):
            back_copy(n, k).wait_recv()
        by, bx = p * 4 + cy, p * 4 + cx
        G[0, by, TOP, :] = (G[0, by, TOP, :].astype(F32) + RD[0, k].astype(F32)).astype(BF)
        GG[by] = (GG[by].astype(F32) + RDg[k].astype(F32)).astype(BF)
        G[0, bx, LOW, :] = (G[0, bx, LOW, :].astype(F32) + RD[1, k].astype(F32)).astype(BF)
        for n in (3, 4, 5, 6):
            back_copy(n, k).start()

    def stores(c, buf):
        cols = pl.ds(pl.multiple_of(c * 256, 256), 256)
        return (
            pltpu.make_async_copy(SG.at[buf], dwg_out.at[cols, :], st_sem.at[0, buf]),
            pltpu.make_async_copy(SU.at[buf], dwu_out.at[cols, :], st_sem.at[1, buf]),
            pltpu.make_async_copy(SD.at[buf], dwd_out.at[:, cols], st_sem.at[2, buf]),
        )

    def weights(c):
        buf = c % 2
        cols = pl.ds(pl.multiple_of(c * 256, 256), 256)

        @pl.when(c >= 2)
        def _():
            for s in stores(c - 2, buf):
                s.wait()

        xt = Xc[:, cols]
        SG[buf] = lax.dot_general(xt, Ac[...], TN, preferred_element_type=F32).astype(BF)
        SU[buf] = lax.dot_general(xt, Bc[...], TN, preferred_element_type=F32).astype(BF)
        SD[buf] = lax.dot_general(Hc[...], Yc[:, cols], TN, preferred_element_type=F32).astype(BF)
        for s in stores(c, buf):
            s.start()

    def third(k):
        p = plane_at(k, z)
        for n in (3, 4, 5, 6):
            back_copy(n, k).wait_recv()
        blk = p * 4 + co
        s = G[0, blk].astype(F32) + RF[0, k].astype(F32) + RF[1, k].astype(F32)
        sg = GG[blk].astype(F32) + RFg[0, k].astype(F32) + RFg[1, k].astype(F32)
        G[0, blk] = s.astype(BF)
        GG[blk] = sg.astype(BF)

        @pl.when(has_up & (p <= z))
        def _():
            line_copy(0, p, True).wait_recv()
            line_copy(1, p, True).wait_recv()
            G[0, blk] = (G[0, blk].astype(F32) + RZ[1, p].astype(F32)).astype(BF)
            GG[blk] = (GG[blk].astype(F32) + RZg[1, p].astype(F32)).astype(BF)

        @pl.when(has_dn & (p >= z))
        def _():
            line_copy(0, p, False).wait_recv()
            line_copy(1, p, False).wait_recv()
            G[0, blk] = (G[0, blk].astype(F32) + RZ[0, p].astype(F32)).astype(BF)
            GG[blk] = (GG[blk].astype(F32) + RZg[0, p].astype(F32)).astype(BF)

        @pl.when(p < z)
        def _():
            line_copy(0, p, True).start()
            line_copy(1, p, True).start()

        @pl.when(p > z)
        def _():
            line_copy(0, p, False).start()
            line_copy(1, p, False).start()

    def rs_step(i, _):
        @pl.when(i < 4)
        def _():
            second(3 - i)
            weights(2 * i)
            weights(2 * i + 1)

        @pl.when(i > 0)
        def _():
            third(4 - i)

        return 0

    lax.fori_loop(0, 5, rs_step, 0)
    gin_out[...] = G[0, me]
    gg_out[...] = GG[me]

    def finish(k, _):
        p = plane_at(k, z)
        for n in range(7):
            back_copy(n, k).wait_send()

        @pl.when(p < z)
        def _():
            line_copy(0, p, True).wait_send()
            line_copy(1, p, True).wait_send()

        @pl.when(p > z)
        def _():
            line_copy(0, p, False).wait_send()
            line_copy(1, p, False).wait_send()

        return 0

    lax.fori_loop(0, 4, finish, 0)
    for c in (6, 7):
        for s in stores(c, c % 2):
            s.wait()


def layer(x, dy, ids_t, g_t, wg, wu, wd):
    tok, width = x.shape
    units = wg.shape[1]
    n = lax.axis_size("expert")
    rows = n * SLOT
    dma = pltpu.SemaphoreType.DMA
    return pl.pallas_call(
        kernel,
        out_shape=(
            jax.ShapeDtypeStruct((tok, width), BF),
            jax.ShapeDtypeStruct((n, tok), BF),
            jax.ShapeDtypeStruct((width, units), BF),
            jax.ShapeDtypeStruct((width, units), BF),
            jax.ShapeDtypeStruct((units, width), BF),
        ),
        in_specs=[pl.BlockSpec(memory_space=pl.ANY)] * 2
        + [pl.BlockSpec(memory_space=pltpu.VMEM)] * 2
        + [pl.BlockSpec(memory_space=pl.ANY)] * 3,
        out_specs=(pl.BlockSpec(memory_space=pltpu.VMEM),) * 2
        + (pl.BlockSpec(memory_space=pl.ANY),) * 3,
        scratch_shapes=[
            pltpu.VMEM((2, n, tok, width), BF),
            pltpu.VMEM((n, 32, tok), BF),
            pltpu.VMEM((rows, width), BF),
            pltpu.VMEM((rows, width), BF),
            pltpu.VMEM((rows, width), BF),
            pltpu.VMEM((rows, units), BF),
            pltpu.VMEM((rows, units), BF),
            pltpu.VMEM((rows, units), BF),
            pltpu.VMEM((width, units), BF),
            pltpu.VMEM((width, units), BF),
            pltpu.VMEM((units, width), BF),
            pltpu.VMEM((n, 16, tok), BF),
            pltpu.VMEM((2, 4, tok, width), BF),
            pltpu.VMEM((2, 4, tok // 2, width), BF),
            pltpu.VMEM((2, 4, tok, width), BF),
            pltpu.VMEM((2, 4, 16, tok), BF),
            pltpu.VMEM((4, 16, tok), BF),
            pltpu.VMEM((2, 4, 16, tok), BF),
            pltpu.VMEM((2, 256, units), BF),
            pltpu.VMEM((2, 256, units), BF),
            pltpu.VMEM((2, units, 256), BF),
            dma((5,)),
            dma((2, n)),
            dma((2, n, 4)),
            dma((n,)),
            dma((n, 4)),
            dma((7, 4)),
            dma((7, 4)),
            dma((2, 2, 4)),
            dma((2, 4)),
            dma((3, 2)),
        ],
        compiler_params=pltpu.CompilerParams(
            collective_id=0, has_side_effects=True, vmem_limit_bytes=64 * 1024 * 1024 - 65536
        ),
        cost_estimate=pl.CostEstimate(flops=33_000_000_000, bytes_accessed=22_000_000, transcendentals=1_000_000),
    )(x, dy, ids_t, g_t, wg, wu, wd)


def on_device(hidden, out_grad, expert_ids, gate_weight, w_gate, w_up, w_down):
    ids_t = expert_ids[0].T
    g_t = gate_weight[0].T.astype(F32)
    grad_in, table, dwg, dwu, dwd = layer(
        hidden[0], out_grad[0], ids_t, g_t, w_gate[0, 0], w_up[0, 0], w_down[0, 0])
    experts = jnp.arange(table.shape[0], dtype=jnp.int32)
    own = ids_t[:, None, :] == experts[None, :, None]
    grad_gate = jnp.sum(jnp.where(own, table[None].astype(F32), 0.0), axis=1).T.astype(BF)
    sections = range(lax.axis_size("section"))
    grad_prev = lax.ppermute(grad_in, "section", [(i + 1, i) for i in sections if i + 1 in sections])
    return grad_prev[None], grad_gate[None], dwg[None, None], dwu[None, None], dwd[None, None]


def solution(mesh):
    wide = P("section", "expert", None)
    deep = P("section", "expert", None, None)
    return jax.shard_map(
        on_device,
        mesh=mesh,
        in_specs=(wide, wide, wide, wide, deep, deep, deep),
        out_specs=(wide, wide, deep, deep, deep),
        check_vma=False,
    )
```

time: 754 us -> 245 us (0.32); the launches traced: 744 us -> 245 us
  waiting for transfers between devices: 234 us -> 0.01 us
  matrix products: 230 us -> 0 us
  Pallas kernels: 0 us -> 225 us
  local copies, waits for them, and re-layouts: 157 us -> 9.39 us
  starting transfers between devices: 89.7 us -> 6.51 us
  other arithmetic: 30.6 us -> 3.24 us
    all_to_all x5 -> x0, waiting for transfers between devices: 234 us -> none  [the longest x1 87 us: on_device(): lax.all_to_all(send_dy, 'expert', split_axis=0, concat_axis=0, tiled=True)]
    dot_general x80 -> x0, matrix products: 230 us -> none  [the longest x10 40 us: expert_rows(): jnp.dot(grad_b, w_up_e.T, preferred_element_type=jnp.float32)]
    pallas_call x0 -> x1, Pallas kernels: none -> 225 us  [layer(): pl.pallas_call(kernel, out_shape=(jax.ShapeDtypeStruct((tok, width), BF),...]
    all_to_all x5 -> x0, starting transfers between devices: 86 us -> none  [the longest x1 24.8 us: on_device(): lax.all_to_all(send_x, 'expert', split_axis=0, concat_axis=0, tiled=True)]
    scatter x6 -> x0, local copies, waits for them, and re-layouts: 67.9 us -> none  [the longest x1 14.2 us: on_device(): jnp.zeros((padded, width), jnp.bfloat16).at[place].set(flat_x, mode='drop')]
    gather x5 -> x0, local copies, waits for them, and re-layouts: 40.9 us -> none  [the longest x1 14 us: on_device(): jnp.take(out_rows, place, axis=0, mode='fill', fill_value=0)]
    while x200 -> x0, local copies, waits for them, and re-layouts: 26.9 us -> none
    broadcast_in_dim x2 -> x0, other arithmetic: 12.9 us -> none  [the longest x1 7.91 us: on_device(): acc_up.astype(jnp.bfloat16)[None, None]]
  transfers between devices with their start and end apart: 6 -> 1, of which waited for: 3 -> 0; matrix products, arithmetic and copies ran while one was open for 13% -> 1% of each run, Pallas kernels for 0% -> 0%
where the time goes in v1:
time: 245 us
  Pallas kernels  225 us (92%)
  local copies, waits for them, and re-layouts  9.39 us (4%)
  starting transfers between devices  6.51 us (3%)
  other arithmetic  3.24 us (1%)
    pallas_call x1, Pallas kernels, layer(): pl.pallas_call(kernel, out_shape=(jax.ShapeDtypeStruct((tok, width), BF),...  225 us
    unnamed x8, local copies, waits for them, and re-layouts  9.39 us
    ppermute x1, starting transfers between devices, on_device(): lax.ppermute(grad_in, 'section', [(i + 1, i) for i in sections if i + 1 i...  6.51 us
  transfers between devices with their start and end apart: 1, of which 0 were waited for; matrix products, arithmetic and copies ran while one was open for 1% of the time, Pallas kernels for 0%

profile of v1, /device:TPU:1, one launch (start us, length us, event | category | flops | bytes accessed | tf_op | source)
XLA Modules:
  0.0 245.1 jit_solution(4445356369779780672)
XLA Ops:
  0.6 1.3 convert_bitcast_fusion.g_t
  1.9 225.3 %shard_map.110 = (bf16[128,2048]{1,0:T(8,128)(2,1)}, bf16[16,128]{1,0:T(8,128)(2,1)}, bf16[2048,768]{1,0:T(8,128)(2,1)}, bf16[2048,768]{1,0:T(8,128)(2,1)}, bf16[768,2048]{1,0:T(8,128)(2,1)}) custom-call(bf16[128,2048]{1,0:T(8,128)(2,1)} %bitcast.32, bf16[128,2048]{1,0:T(8,128)(2,1)} %bitcast.33, s32[8,128]{1,0:T(8,128)} %bitcast.26, ...), custom_call_target="tpu_custom_call" | custom-call | flops 32999999488 | bytes 22000000 | tf_op jit(solution)/shard_map/pallas_call | solution.py:405
  227.2 6.5 %collective-permute-start = (bf16[128,2048]{1,0:T(8,128)(2,1)}, bf16[128,2048]{1,0:T(8,128)(2,1)S(1)}, u32[]{:S(2)}, u32[]{:S(2)}) collective-permute-start(bf16[128,2048]{1,0:T(8,128)(2,1)} %get-tuple-element.10), channel_id=1, source_target_pairs={{16,0},{17,1},{18,2},{19,3},{20,4},{21,5},{22,6},{23,7},{24,8},{25... | collective-permute-start | bytes 1572872 | tf_op jit(solution)/shard_map/ppermute | solution.py:468
  233.7 0.7 convert_element_type.20
  234.4 1.3 select_reduce_fusion
  235.7 0.0 collective-permute-done
  235.7 0.8 copy.16
  236.5 0.0 copy-start.1
  236.5 3.9 %copy.17 = bf16[1,1,2048,768]{3,2,1,0:T(8,128)(2,1)} copy(bf16[1,1,2048,768]{3,2,1,0:T(8,128)(2,1)} %bitcast.24) | data formatting | bytes 6291456
  240.4 0.0 copy-done.1
  240.4 0.0 copy-start
  240.4 1.7 copy.18
  242.0 1.4 copy-done
  243.4 1.7 copy.19
Async XLA Ops:
  227.2 8.5 %collective-permute-start = (bf16[128,2048]{1,0:T(8,128)(2,1)}, bf16[128,2048]{1,0:T(8,128)(2,1)S(1)}, u32[]{:S(2)}, u32[]{:S(2)}) collective-permute-start(bf16[128,2048]{1,0:T(8,128)(2,1)} %get-tuple-element.10), channel_id=1, source_target_pairs={{16,0},{17,1},{18,2},{19,3},{20,4},{21,5},{22,6},{23,7},{24,8},{25... | collective-permute-start | bytes 1572872 | tf_op jit(solution)/shard_map/ppermute | solution.py:468
  236.5 3.9 %copy-start.1 = (bf16[2048,768]{1,0:T(8,128)(2,1)S(1)}, bf16[2048,768]{1,0:T(8,128)(2,1)}, u32[]{:S(2)}) copy-start(bf16[2048,768]{1,0:T(8,128)(2,1)} %get-tuple-element.13) | copy-start | bytes 9437188
  240.4 3.0 %copy-start = (bf16[768,2048]{1,0:T(8,128)(2,1)S(1)}, bf16[768,2048]{1,0:T(8,128)(2,1)}, u32[]{:S(2)}) copy-start(bf16[768,2048]{1,0:T(8,128)(2,1)} %get-tuple-element.14) | copy-start | bytes 9437188

commit v2 on v1

--- a/solution.py
+++ b/solution.py
@@ -26,9 +26,9 @@
 def kernel(
     x_in, dy_in, ids_t, g_t, wg_in, wu_in, wd_in,
     gin_out, gg_out, dwg_out, dwu_out, dwd_out,
-    G, META, Xc, Yc, Dx, Hc, Ac, Bc, wg, wu, wd, GG, RF, RD, RZ, RFg, RDg, RZg, SG, SU, SD,
+    G, META, Xc, Yc, Dx, Hc, Ac, Bc, wg, wu, wd, GG, SX, RL, BK, RB, RZ, RFg, RGg, RZg, SG, SU, SD,
     load_sem, in_sem, out_sem, in_meta, out_meta,
-    rs_in, rs_out, rz_in, rz_out, st_sem,
+    side_in, side_out, rs_in, rs_out, rz_in, rz_out, st_sem,
 ):
     tok, width = x_in.shape
     units = wg.shape[1]
@@ -48,7 +48,7 @@
 
     loads = []
     for n, (src, dst) in enumerate(
-        ((x_in, G.at[0, me]), (dy_in, G.at[1, me]), (wg_in, wg), (wu_in, wu), (wd_in, wd))
+        ((x_in, G.at[0, z]), (dy_in, G.at[1, z]), (wg_in, wg), (wu_in, wu), (wd_in, wd))
     ):
         c = pltpu.make_async_copy(src, dst, load_sem.at[n])
         c.start()
@@ -83,92 +83,163 @@
 
     pl.semaphore_wait(barrier, 2 + (5 - z) // 3 + (z + 2) // 3)
 
-    def block_copy(arr, blk, way, to):
-        if arr == 2:
-            return pltpu.make_async_remote_copy(
-                META.at[blk], META.at[blk], out_meta.at[blk, way], in_meta.at[blk],
-                device_id=to, device_id_type=MESH)
+    def line(arr, p, way, to):
         return pltpu.make_async_remote_copy(
-            G.at[arr, blk], G.at[arr, blk], out_sem.at[arr, blk, way], in_sem.at[arr, blk],
+            G.at[arr, p], G.at[arr, p], out_sem.at[arr, p, way], in_sem.at[arr, p],
             device_id=to, device_id_type=MESH)
 
-    def arrive(arr, blk):
-        block_copy(arr, blk, 0, to_x).wait_recv()
+    def meta(blk, way, to):
+        return pltpu.make_async_remote_copy(
+            META.at[blk], META.at[blk], out_meta.at[blk, way], in_meta.at[blk],
+            device_id=to, device_id_type=MESH)
+
+    def part(k, i):
+        return pl.ds(pl.multiple_of(k * (4 * SLOT) + i * SLOT, SLOT), SLOT)
+
+    def side(n, k):
+        src, dst, to = (
+            (SX.at[0, 0, k], Xc.at[part(k, 1), :], to_x),
+            (SX.at[1, 0, k], Yc.at[part(k, 1), :], to_x),
+            (SX.at[0, 1, k], Xc.at[part(k, 2), :], to_y),
+            (SX.at[1, 1, k], Yc.at[part(k, 2), :], to_y),
+            (SX.at[0, 2, k], RL.at[0, k], to_x),
+            (SX.at[1, 2, k], RL.at[1, k], to_y),
+            (RL.at[0, k], Xc.at[part(k, 3), :], to_y),
+            (RL.at[1, k], Yc.at[part(k, 3), :], to_x),
+        )[n]
+        return pltpu.make_async_remote_copy(
+            src, dst, side_out.at[n, k], side_in.at[n, k], device_id=to, device_id_type=MESH)
+
+    expert_row = lax.broadcasted_iota(jnp.int32, (16, tok), 0)
+
+    def table_row(blk, first, expert):
+        rows = META[blk, first : first + 16, :].astype(F32)
+        return jnp.sum(jnp.where(expert_row == expert, rows, 0.0), axis=0, keepdims=True)
+
+    def onehot(blk, expert):
+        slots = lax.broadcasted_iota(jnp.int32, (SLOT, tok), 0).astype(F32)
+        return (slots == table_row(blk, 0, expert)).astype(F32)
+
+    def compact(k):
+        p = plane_at(k, z)
+        for i, c in ((3, cd), (1, cx), (2, cy), (0, co)):
+            pb = onehot(p * 4 + co, z * 4 + c).astype(BF)
+
+            def pack(j, _, pb=pb, i=i):
+                cols = pl.ds(pl.multiple_of(j * 512, 512), 512)
+                px = jnp.dot(pb, G[0, p, :, cols], preferred_element_type=F32).astype(BF)
+                py = jnp.dot(pb, G[1, p, :, cols], preferred_element_type=F32).astype(BF)
+                if i == 0:
+                    Xc[part(k, 0), cols] = px
+                    Yc[part(k, 0), cols] = py
+                else:
+                    SX[0, i - 1, k, :, cols] = px
+                    SX[1, i - 1, k, :, cols] = py
+                return 0
+
+            lax.fori_loop(0, width // 512, pack, 0)
+            for n in ((), (0, 1), (2, 3), (4, 5))[i]:
+                side(n, k).start()
 
     loads[0].wait()
     loads[1].wait()
 
-    for arr in (2, 0, 1):
-        @pl.when(has_up)
-        def _(arr=arr):
-            block_copy(arr, me, 2, to_up).start()
-
-        @pl.when(has_dn)
-        def _(arr=arr):
-            block_copy(arr, me, 3, to_dn).start()
-
-        block_copy(arr, me, 0, to_x).start()
-        block_copy(arr, me, 1, to_y).start()
+    @pl.when(has_up)
+    def _():
+        meta(me, 2, to_up).start()
+        line(0, z, 0, to_up).start()
+        line(1, z, 0, to_up).start()
+
+    @pl.when(has_dn)
+    def _():
+        meta(me, 3, to_dn).start()
+        line(0, z, 1, to_dn).start()
+        line(1, z, 1, to_dn).start()
+
+    meta(me, 0, to_x).start()
+    meta(me, 1, to_y).start()
+    compact(0)
     for c in loads[2:]:
         c.wait()
 
     def own_step(k):
         p = plane_at(k, z)
         blk = p * 4 + co
-        for arr in (2, 0, 1):
-            arrive(arr, blk)
+        meta(blk, 0, to_x).wait_recv()
+
+        @pl.when((p > z) & has_dn)
+        def _():
+            meta(blk, 3, to_dn).start()
+
+        @pl.when((p < z) & has_up)
+        def _():
+            meta(blk, 2, to_up).start()
+
+        meta(blk, 0, to_x).start()
+        meta(blk, 1, to_y).start()
+        for arr in (0, 1):
+            line(arr, p, 0, to_up).wait_recv()
 
             @pl.when((p > z) & has_dn)
             def _(arr=arr):
-                block_copy(arr, blk, 3, to_dn).start()
+                line(arr, p, 1, to_dn).start()
 
             @pl.when((p < z) & has_up)
             def _(arr=arr):
-                block_copy(arr, blk, 2, to_up).start()
-
-            block_copy(arr, blk, 0, to_x).start()
-            block_copy(arr, blk, 1, to_y).start()
+                line(arr, p, 0, to_up).start()
+
+        compact(k)
 
     def side_step(k):
         p = plane_at(k, z)
-        for arr in (2, 0, 1):
-            arrive(arr, p * 4 + cx)
-            if arr != 1:
-                block_copy(arr, p * 4 + cx, 1, to_y).start()
-            arrive(arr, p * 4 + cy)
-            if arr == 1:
-                block_copy(arr, p * 4 + cy, 0, to_x).start()
-
-    expert_row = lax.broadcasted_iota(jnp.int32, (16, tok), 0) == me
-
-    def onehot(blk):
-        r = jnp.sum(jnp.where(expert_row, META[blk, 0:16, :].astype(F32), 0.0), axis=0, keepdims=True)
-        slots = lax.broadcasted_iota(jnp.int32, (SLOT, tok), 0).astype(F32)
-        return (slots == r).astype(F32)
+        meta(p * 4 + cx, 0, to_x).wait_recv()
+        meta(p * 4 + cx, 1, to_y).start()
+        side(4, k).wait_recv()
+        side(6, k).start()
+        side(5, k).wait_recv()
+        side(7, k).start()
+        meta(p * 4 + cy, 0, to_x).wait_recv()
+
+    LEFT, RIGHT = pl.ds(0, width // 2), pl.ds(width // 2, width // 2)
+
+    def back_copy(n, k):
+        p = plane_at(k, z)
+        slot = [pl.ds(i * SLOT, SLOT) for i in range(3)]
+        src, dst, to = (
+            (Dx.at[part(k, 1), :], BK.at[k, slot[0], :], to_x),
+            (Dx.at[part(k, 2), :], BK.at[k, slot[1], :], to_y),
+            (Dx.at[part(k, 3), LEFT], RB.at[0, k], to_x),
+            (Dx.at[part(k, 3), RIGHT], RB.at[1, k], to_y),
+            (RB.at[0, k], BK.at[k, slot[2], LEFT], to_y),
+            (RB.at[1, k], BK.at[k, slot[2], RIGHT], to_x),
+            (GG.at[p * 4 + cx], RFg.at[0, k], to_x),
+            (GG.at[p * 4 + cy], RFg.at[1, k], to_y),
+            (GG.at[p * 4 + cd], RGg.at[k], to_x),
+            (RGg.at[k], RFg.at[2, k], to_y),
+        )[n]
+        return pltpu.make_async_remote_copy(
+            src, dst, rs_out.at[n, k], rs_in.at[n, k], device_id=to, device_id_type=MESH)
+
+    def send_back(k):
+        for n in (2, 3, 8, 6, 7, 0, 1):
+            back_copy(n, k).start()
 
     def group(k):
         p = plane_at(k, z)
-        for arr in (2, 0, 1):
-            arrive(arr, p * 4 + cd)
-        base = k * (4 * SLOT)
-        rows = pl.ds(pl.multiple_of(base, 4 * SLOT), 4 * SLOT)
+        meta(p * 4 + cd, 0, to_x).wait_recv()
+        for n in (0, 1, 2, 3, 6, 7):
+            side(n, k).wait_recv()
+
+        @pl.when(k == 3)
+        def _():
+            send_back(0)
+
+        rows = pl.ds(pl.multiple_of(k * (4 * SLOT), 4 * SLOT), 4 * SLOT)
         scales, picks = [], []
-        for i, c in enumerate((co, cx, cy, cd)):
-            blk = p * 4 + c
-            pick = onehot(blk)
-            gs = jnp.sum(jnp.where(expert_row, META[blk, 16:32, :].astype(F32), 0.0), axis=0, keepdims=True)
-            scales.append(jnp.sum(pick * gs, axis=1, keepdims=True))
+        for c in (co, cx, cy, cd):
+            pick = onehot(p * 4 + c, me)
+            scales.append(jnp.sum(pick * table_row(p * 4 + c, 16, me), axis=1, keepdims=True))
             picks.append(pick)
-            part = pl.ds(pl.multiple_of(base + i * SLOT, SLOT), SLOT)
-            pb = pick.astype(BF)
-
-            def gather(j, _, pb=pb, blk=blk, part=part):
-                cols = pl.ds(pl.multiple_of(j * 512, 512), 512)
-                Xc[part, cols] = jnp.dot(pb, G[0, blk, :, cols], preferred_element_type=F32).astype(BF)
-                Yc[part, cols] = jnp.dot(pb, G[1, blk, :, cols], preferred_element_type=F32).astype(BF)
-                return 0
-
-            lax.fori_loop(0, width // 512, gather, 0)
         scale = jnp.concatenate(scales, axis=0)
 
         def hidden_chunk(j, total):
@@ -188,7 +259,7 @@
         total = lax.fori_loop(0, units // 256, hidden_chunk, jnp.zeros((4 * SLOT, 1), F32))
         for i, c in enumerate((co, cx, cy, cd)):
             row = jnp.sum(picks[i] * total[i * SLOT : (i + 1) * SLOT], axis=0, keepdims=True)
-            GG[p * 4 + c] = jnp.where(expert_row, row, 0.0).astype(BF)
+            GG[p * 4 + c] = jnp.where(expert_row == me, row, 0.0).astype(BF)
 
         def input_chunk(j, _):
             cols = pl.ds(pl.multiple_of(j * 256, 256), 256)
@@ -217,86 +288,49 @@
 
     lax.fori_loop(0, 5, ag_step, 0)
 
+    for k in (3, 2, 1):
+        send_back(k)
+
     def drain(k, _):
         p = plane_at(k, z)
         blk = p * 4 + co
-        for arr in (0, 1, 2):
-            block_copy(arr, blk, 0, to_x).wait_send()
-            block_copy(arr, blk, 1, to_y).wait_send()
-
-            @pl.when(has_up & (p <= z))
-            def _(arr=arr):
-                block_copy(arr, blk, 2, to_up).wait_send()
-
-            @pl.when(has_dn & (p >= z))
-            def _(arr=arr):
-                block_copy(arr, blk, 3, to_dn).wait_send()
-
-            if arr != 1:
-                block_copy(arr, p * 4 + cx, 1, to_y).wait_send()
-            else:
-                block_copy(arr, p * 4 + cy, 0, to_x).wait_send()
+        meta(blk, 0, to_x).wait_send()
+        meta(blk, 1, to_y).wait_send()
+        meta(p * 4 + cx, 1, to_y).wait_send()
+        for n in range(8):
+            side(n, k).wait_send()
+
+        @pl.when(has_up & (p <= z))
+        def _():
+            meta(blk, 2, to_up).wait_send()
+            for arr in (0, 1):
+                line(arr, p, 0, to_up).wait_send()
+
+        @pl.when(has_dn & (p >= z))
+        def _():
+            meta(blk, 3, to_dn).wait_send()
+            for arr in (0, 1):
+                line(arr, p, 1, to_dn).wait_send()
+
         return 0
 
     lax.fori_loop(0, 4, drain, 0)
-
-    halves = tok // 2
-    TOP, LOW = pl.ds(0, halves), pl.ds(halves, halves)
-
-    def back_copy(n, k):
-        p = plane_at(k, z)
-        src, dst, to = (
-            (G.at[0, p * 4 + cd, TOP, :], RD.at[0, k], to_x),
-            (G.at[0, p * 4 + cd, LOW, :], RD.at[1, k], to_y),
-            (GG.at[p * 4 + cd], RDg.at[k], to_x),
-            (G.at[0, p * 4 + cx], RF.at[0, k], to_x),
-            (G.at[0, p * 4 + cy], RF.at[1, k], to_y),
-            (GG.at[p * 4 + cx], RFg.at[0, k], to_x),
-            (GG.at[p * 4 + cy], RFg.at[1, k], to_y),
-        )[n]
-        return pltpu.make_async_remote_copy(
-            src, dst, rs_out.at[n, k], rs_in.at[n, k], device_id=to, device_id_type=MESH)
 
     def line_copy(n, t, down):
         blk = t * 4 + co
         d = 1 if down else 0
-        src, dst = ((G.at[0, blk], RZ.at[d, t]), (GG.at[blk], RZg.at[d, t]))[n]
+        src, dst = ((G.at[0, t], RZ.at[d, t]), (GG.at[blk], RZg.at[d, t]))[n]
         return pltpu.make_async_remote_copy(
             src, dst, rz_out.at[n, t], rz_in.at[n, d, t],
             device_id=to_dn if down else to_up, device_id_type=MESH)
 
-    def spread(i, _):
-        k = 3 - i
-        p = plane_at(k, z)
-        for n, c in ((3, cd), (1, cx), (2, cy), (0, co)):
-            blk = p * 4 + c
-            pb = onehot(blk).astype(BF)
-            part = pl.ds(pl.multiple_of(k * (4 * SLOT) + n * SLOT, SLOT), SLOT)
-
-            def put(j, _, pb=pb, blk=blk, part=part):
-                cols = pl.ds(pl.multiple_of(j * 512, 512), 512)
-                G[0, blk, :, cols] = lax.dot_general(
-                    pb, Dx[part, cols], TN, preferred_element_type=F32).astype(BF)
-                return 0
-
-            lax.fori_loop(0, width // 512, put, 0)
-            if n == 3:
-                for m in (0, 1, 2):
-                    back_copy(m, k).start()
-        return 0
-
-    lax.fori_loop(0, 4, spread, 0)
-
     def second(k):
-        p = plane_at(k, z)
-        for n in (0, 1, 2):
-            back_copy(n, k).wait_recv()
-        by, bx = p * 4 + cy, p * 4 + cx
-        G[0, by, TOP, :] = (G[0, by, TOP, :].astype(F32) + RD[0, k].astype(F32)).astype(BF)
-        GG[by] = (GG[by].astype(F32) + RDg[k].astype(F32)).astype(BF)
-        G[0, bx, LOW, :] = (G[0, bx, LOW, :].astype(F32) + RD[1, k].astype(F32)).astype(BF)
-        for n in (3, 4, 5, 6):
-            back_copy(n, k).start()
+        back_copy(2, k).wait_recv()
+        back_copy(4, k).start()
+        back_copy(3, k).wait_recv()
+        back_copy(5, k).start()
+        back_copy(8, k).wait_recv()
+        back_copy(9, k).start()
 
     def stores(c, buf):
         cols = pl.ds(pl.multiple_of(c * 256, 256), 256)
@@ -324,26 +358,37 @@
 
     def third(k):
         p = plane_at(k, z)
-        for n in (3, 4, 5, 6):
+        for n in (0, 1, 4, 5, 6, 7, 9):
             back_copy(n, k).wait_recv()
         blk = p * 4 + co
-        s = G[0, blk].astype(F32) + RF[0, k].astype(F32) + RF[1, k].astype(F32)
-        sg = GG[blk].astype(F32) + RFg[0, k].astype(F32) + RFg[1, k].astype(F32)
-        G[0, blk] = s.astype(BF)
+        first = onehot(blk, me).astype(BF)
+        rest = jnp.concatenate([onehot(blk, z * 4 + c) for c in (cx, cy, cd)], axis=0).astype(BF)
+
+        def spread(j, _):
+            cols = pl.ds(pl.multiple_of(j * 512, 512), 512)
+            total = lax.dot_general(first, Dx[part(k, 0), cols], TN, preferred_element_type=F32)
+            total = total + lax.dot_general(rest, BK[k, :, cols], TN, preferred_element_type=F32)
+            G[0, p, :, cols] = total.astype(BF)
+            return 0
+
+        lax.fori_loop(0, width // 512, spread, 0)
+        sg = GG[blk].astype(F32)
+        for n in range(3):
+            sg = sg + RFg[n, k].astype(F32)
         GG[blk] = sg.astype(BF)
 
         @pl.when(has_up & (p <= z))
         def _():
             line_copy(0, p, True).wait_recv()
             line_copy(1, p, True).wait_recv()
-            G[0, blk] = (G[0, blk].astype(F32) + RZ[1, p].astype(F32)).astype(BF)
+            G[0, p] = (G[0, p].astype(F32) + RZ[1, p].astype(F32)).astype(BF)
             GG[blk] = (GG[blk].astype(F32) + RZg[1, p].astype(F32)).astype(BF)
 
         @pl.when(has_dn & (p >= z))
         def _():
             line_copy(0, p, False).wait_recv()
             line_copy(1, p, False).wait_recv()
-            G[0, blk] = (G[0, blk].astype(F32) + RZ[0, p].astype(F32)).astype(BF)
+            G[0, p] = (G[0, p].astype(F32) + RZ[0, p].astype(F32)).astype(BF)
             GG[blk] = (GG[blk].astype(F32) + RZg[0, p].astype(F32)).astype(BF)
 
         @pl.when(p < z)
@@ -370,12 +415,12 @@
         return 0
 
     lax.fori_loop(0, 5, rs_step, 0)
-    gin_out[...] = G[0, me]
+    gin_out[...] = G[0, z]
     gg_out[...] = GG[me]
 
     def finish(k, _):
         p = plane_at(k, z)
-        for n in range(7):
+        for n in range(10):
             back_copy(n, k).wait_send()
 
         @pl.when(p < z)
@@ -417,7 +462,7 @@
         out_specs=(pl.BlockSpec(memory_space=pltpu.VMEM),) * 2
         + (pl.BlockSpec(memory_space=pl.ANY),) * 3,
         scratch_shapes=[
-            pltpu.VMEM((2, n, tok, width), BF),
+            pltpu.VMEM((2, 4, tok, width), BF),
             pltpu.VMEM((n, 32, tok), BF),
             pltpu.VMEM((rows, width), BF),
             pltpu.VMEM((rows, width), BF),
@@ -429,22 +474,26 @@
             pltpu.VMEM((width, units), BF),
             pltpu.VMEM((units, width), BF),
             pltpu.VMEM((n, 16, tok), BF),
+            pltpu.VMEM((2, 3, 4, SLOT, width), BF),
+            pltpu.VMEM((2, 4, SLOT, width), BF),
+            pltpu.VMEM((4, 3 * SLOT, width), BF),
+            pltpu.VMEM((2, 4, SLOT, width // 2), BF),
             pltpu.VMEM((2, 4, tok, width), BF),
-            pltpu.VMEM((2, 4, tok // 2, width), BF),
-            pltpu.VMEM((2, 4, tok, width), BF),
-            pltpu.VMEM((2, 4, 16, tok), BF),
+            pltpu.VMEM((3, 4, 16, tok), BF),
             pltpu.VMEM((4, 16, tok), BF),
             pltpu.VMEM((2, 4, 16, tok), BF),
             pltpu.VMEM((2, 256, units), BF),
             pltpu.VMEM((2, 256, units), BF),
             pltpu.VMEM((2, units, 256), BF),
             dma((5,)),
-            dma((2, n)),
-            dma((2, n, 4)),
+            dma((2, 4)),
+            dma((2, 4, 2)),
             dma((n,)),
             dma((n, 4)),
-            dma((7, 4)),
-            dma((7, 4)),
+            dma((8, 4)),
+            dma((8, 4)),
+            dma((10, 4)),
+            dma((10, 4)),
             dma((2, 2, 4)),
             dma((2, 4)),
             dma((3, 2)),

time: 245 us -> 229 us (0.935)
  Pallas kernels: 225 us -> 196 us
  starting transfers between devices: 6.51 us -> 20.2 us
    pallas_call x1, Pallas kernels: 225 us -> 196 us  [layer(): pl.pallas_call(kernel, out_shape=(jax.ShapeDtypeStruct((tok, width), BF),...]
    ppermute x1, starting transfers between devices: 6.51 us -> 20.2 us  [on_device(): lax.ppermute(grad_in, 'section', [(i + 1, i) for i in sections if i + 1 i...]
where the time goes in v2:
time: 229 us
  Pallas kernels  196 us (86%)
  starting transfers between devices  20.2 us (9%)
  local copies, waits for them, and re-layouts  9.39 us (4%)
  other arithmetic  3.24 us (1%)
    pallas_call x1, Pallas kernels, layer(): pl.pallas_call(kernel, out_shape=(jax.ShapeDtypeStruct((tok, width), BF),...  196 us
    ppermute x1, starting transfers between devices, on_device(): lax.ppermute(grad_in, 'section', [(i + 1, i) for i in sections if i + 1 i...  20.2 us
    unnamed x8, local copies, waits for them, and re-layouts  9.39 us
  transfers between devices with their start and end apart: 1, of which 0 were waited for; matrix products, arithmetic and copies ran while one was open for 1% of the time, Pallas kernels for 0%

profile of v2, /device:TPU:1, one launch (start us, length us, event | category | flops | bytes accessed | tf_op | source)
XLA Modules:
  0.0 229.1 jit_solution(12670898290022957651)
XLA Ops:
  0.6 1.3 convert_bitcast_fusion.g_t
  1.9 195.6 %shard_map.110 = (bf16[128,2048]{1,0:T(8,128)(2,1)}, bf16[16,128]{1,0:T(8,128)(2,1)}, bf16[2048,768]{1,0:T(8,128)(2,1)}, bf16[2048,768]{1,0:T(8,128)(2,1)}, bf16[768,2048]{1,0:T(8,128)(2,1)}) custom-call(bf16[128,2048]{1,0:T(8,128)(2,1)} %bitcast.32, bf16[128,2048]{1,0:T(8,128)(2,1)} %bitcast.33, s32[8,128]{1,0:T(8,128)} %bitcast.26, ...), custom_call_target="tpu_custom_call" | custom-call | flops 32999999488 | bytes 22000000 | tf_op jit(solution)/shard_map/pallas_call | solution.py:450
  197.5 20.2 %collective-permute-start = (bf16[128,2048]{1,0:T(8,128)(2,1)}, bf16[128,2048]{1,0:T(8,128)(2,1)S(1)}, u32[]{:S(2)}, u32[]{:S(2)}) collective-permute-start(bf16[128,2048]{1,0:T(8,128)(2,1)} %get-tuple-element.10), channel_id=1, source_target_pairs={{16,0},{17,1},{18,2},{19,3},{20,4},{21,5},{22,6},{23,7},{24,8},{25... | collective-permute-start | bytes 1572872 | tf_op jit(solution)/shard_map/ppermute | solution.py:517
  217.7 0.7 convert_element_type.20
  218.4 1.3 select_reduce_fusion
  219.7 0.0 collective-permute-done
  219.7 0.8 copy.16
  220.5 0.0 copy-start.1
  220.5 3.9 %copy.17 = bf16[1,1,2048,768]{3,2,1,0:T(8,128)(2,1)} copy(bf16[1,1,2048,768]{3,2,1,0:T(8,128)(2,1)} %bitcast.24) | data formatting | bytes 6291456
  224.4 0.0 copy-done.1
  224.4 0.0 copy-start
  224.4 1.7 copy.18
  226.0 1.4 copy-done
  227.4 1.7 copy.19
Async XLA Ops:
  197.5 22.2 %collective-permute-start = (bf16[128,2048]{1,0:T(8,128)(2,1)}, bf16[128,2048]{1,0:T(8,128)(2,1)S(1)}, u32[]{:S(2)}, u32[]{:S(2)}) collective-permute-start(bf16[128,2048]{1,0:T(8,128)(2,1)} %get-tuple-element.10), channel_id=1, source_target_pairs={{16,0},{17,1},{18,2},{19,3},{20,4},{21,5},{22,6},{23,7},{24,8},{25... | collective-permute-start | bytes 1572872 | tf_op jit(solution)/shard_map/ppermute | solution.py:517
  220.5 3.9 %copy-start.1 = (bf16[2048,768]{1,0:T(8,128)(2,1)S(1)}, bf16[2048,768]{1,0:T(8,128)(2,1)}, u32[]{:S(2)}) copy-start(bf16[2048,768]{1,0:T(8,128)(2,1)} %get-tuple-element.13) | copy-start | bytes 9437188
  224.4 3.0 %copy-start = (bf16[768,2048]{1,0:T(8,128)(2,1)S(1)}, bf16[768,2048]{1,0:T(8,128)(2,1)}, u32[]{:S(2)}) copy-start(bf16[768,2048]{1,0:T(8,128)(2,1)} %get-tuple-element.14) | copy-start | bytes 9437188
